TPU v7x, 32 devices: a whole 2x2x4 slice. The times are simulated.
32 devices in a mesh: pipe: 4 (over y, core), section: 2 (over x), tp: 4 (over z).
Axes of the slice: x: 2, y: 2, z: 4, core: 2. Of those that a mesh axis runs over, the one named last changes fastest.
Arguments:
- weights: bfloat16 [4, 2, 2, 4096, 512], P('pipe', 'section', None, 'tp'), may hold values from -6 to 6
- first_moment: float32 [4, 2, 2, 4096, 512], P('pipe', 'section', None, 'tp'), may hold values from -4 to 4
- second_moment: float32 [4, 2, 2, 4096, 512], P('pipe', 'section', None, 'tp'), may hold values from 0.1 to 2
- gradients: bfloat16 [4, 2, 2, 4096, 512], P('pipe', 'section', None, 'tp'), may hold values from -6 to 6
- old_section: int32 [4, 3], replicated, may hold values from 0 to 1, as said below
- new_section: int32 [3], replicated, may hold values from 0 to 1, as said below
- lost_pipe: int32 [4], replicated, may hold values from 0 to 3, each once
- donor_offset: int32 [3], replicated, may hold values from 1 to 3
Outputs:
- new_weights: bfloat16 [4, 2, 2, 4096, 512], P('pipe', 'section', None, 'tp')
- new_first: float32 [4, 2, 2, 4096, 512], P('pipe', 'section', None, 'tp')
- new_second: float32 [4, 2, 2, 4096, 512], P('pipe', 'section', None, 'tp')
Inputs may be any that keep to these rules, and one draw needn't show every extreme that they name: `old_section`: each row places layers in section order (a layer's section never falls with the layer); 1 section of each row hold exactly 2 layers and the others one each. `new_section`: layers in any order; no section holds more than 2 layers, and some section holds exactly 2.
All inputs are finite; a program needn't handle non-finite values.
Results may differ from a plain program's by a relative error of at most 0.0075.
Values may be sent and summed in bfloat16 or wider, within the bound.
No kernel may reach another device: no remote copies, remote signals or barrier semaphores. Data moves between devices by JAX's collectives and lax.ppermute only.
A program may use at most 64 MiB of HBM per device.

v0:
```python
import jax
import jax.numpy as jnp
from jax import lax
from jax.sharding import PartitionSpec as P

LEARN_RATE = 0.01
BETA_ONE = 0.9
BETA_TWO = 0.95
EPSILON = 1e-08
DECAY_RATE = 0.1


def slot_ranks(section_map):
    layer_ids = jnp.arange(section_map.shape[-1], dtype=jnp.int32)
    same_section = section_map[..., :, None] == section_map[..., None, :]
    before = layer_ids[None, :] < layer_ids[:, None]
    return jnp.sum((same_section & before).astype(jnp.int32), axis=-1)


def per_device(
    weights,
    first_moment,
    second_moment,
    gradients,
    old_section,
    new_section,
    lost_pipe,
    donor_offset,
):
    pipe_total = lax.axis_size("pipe")
    section_total = lax.axis_size("section")
    slot_count = weights.shape[2]
    layer_count = new_section.shape[0]
    held_state = (weights[0, 0], first_moment[0, 0], second_moment[0, 0], gradients[0, 0])
    spread = (
        lax.all_to_all(held_state[0], ("pipe", "section"), split_axis=1, concat_axis=0, tiled=True),
        lax.all_to_all(
            held_state[1].astype(jnp.bfloat16),
            ("pipe", "section"),
            split_axis=1,
            concat_axis=0,
            tiled=True,
        ).astype(jnp.float32),
        lax.all_to_all(
            held_state[2].astype(jnp.bfloat16),
            ("pipe", "section"),
            split_axis=1,
            concat_axis=0,
            tiled=True,
        ).astype(jnp.float32),
        lax.all_to_all(held_state[3], ("pipe", "section"), split_axis=1, concat_axis=0, tiled=True),
    )
    piece_weight, piece_one, piece_two, piece_grad = spread

    def incoming(pipe_at, section_at, slot_at):
        return (pipe_at * section_total + section_at) * slot_count + slot_at

    pipe_ids = jnp.arange(pipe_total, dtype=jnp.int32)
    layer_ids = jnp.arange(layer_count, dtype=jnp.int32)
    is_lost = pipe_ids == lost_pipe[0]
    now_section = jnp.where(is_lost[:, None], new_section[None, :], old_section)
    now_slot = slot_ranks(now_section)
    old_slot = slot_ranks(old_section)
    donors = lost_pipe[donor_offset]
    source = jnp.where(is_lost[:, None], donors[None, :], pipe_ids[:, None])
    source_section = old_section[source, layer_ids[None, :]]
    source_slot = old_slot[source, layer_ids[None, :]]
    grad_index = incoming(pipe_ids[:, None], now_section, now_slot)
    grad_rows = piece_grad[grad_index].astype(jnp.float32)
    mean_grad = jnp.sum(grad_rows, axis=0) / pipe_total
    source_index = incoming(source, source_section, source_slot)
    weight_now = piece_weight[source_index].astype(jnp.float32)
    moment_one = piece_one[source_index]
    moment_two = piece_two[source_index]
    next_one = BETA_ONE * moment_one + (1.0 - BETA_ONE) * mean_grad[None]
    next_two = BETA_TWO * moment_two + (1.0 - BETA_TWO) * mean_grad[None] * mean_grad[None]
    update = next_one / (jnp.sqrt(next_two) + EPSILON) + DECAY_RATE * weight_now
    next_weight = (weight_now - LEARN_RATE * update).astype(jnp.bfloat16)
    place_index = (pipe_ids[:, None] * section_total + now_section) * slot_count + now_slot
    out_weight = jnp.zeros(piece_weight.shape, jnp.bfloat16).at[place_index].set(next_weight)
    out_one = jnp.zeros(piece_one.shape, jnp.float32).at[place_index].set(next_one)
    out_two = jnp.zeros(piece_two.shape, jnp.float32).at[place_index].set(next_two)
    returned = (
        lax.all_to_all(out_weight, ("pipe", "section"), split_axis=0, concat_axis=1, tiled=True),
        lax.all_to_all(
            out_one.astype(jnp.bfloat16),
            ("pipe", "section"),
            split_axis=0,
            concat_axis=1,
            tiled=True,
        ).astype(out_one.dtype),
        lax.all_to_all(
            out_two.astype(jnp.bfloat16),
            ("pipe", "section"),
            split_axis=0,
            concat_axis=1,
            tiled=True,
        ).astype(out_two.dtype),
    )
    final_weight, final_one, final_two = returned
    return (final_weight[None, None], final_one[None, None], final_two[None, None])


def solution(mesh):
    in_specs = (
        P("pipe", "section", None, "tp", None),
        P("pipe", "section", None, "tp", None),
        P("pipe", "section", None, "tp", None),
        P("pipe", "section", None, "tp", None),
        P(),
        P(),
        P(),
        P(),
    )
    out_specs = (
        P("pipe", "section", None, "tp", None),
        P("pipe", "section", None, "tp", None),
        P("pipe", "section", None, "tp", None),
    )
    return jax.shard_map(
        per_device, mesh=mesh, in_specs=in_specs, out_specs=out_specs, check_vma=False
    )
```

profile of v0, /device:TPU:0, one launch (start us, length us, event | category | flops | bytes accessed | tf_op | source)
XLA Modules:
  0.0 251.8 jit_solution(6403699552778442334)
XLA Ops:
  0.6 2.5 convert_element_type.136
  3.1 3.5 %copy.79 = bf16[1,1,2,1024,512]{4,2,3,1,0:T(2,128)(2,1)} copy(bf16[1,1,2,1024,512]{4,3,2,1,0:T(8,128)(2,1)S(1)} %convert_element_type.136) | data formatting | bytes 4194304
  6.6 5.2 %all-to-all-start.1 = ((bf16[2,1024,512]{2,0,1:T(2,128)(2,1)}), bf16[2,1024,512]{2,0,1:T(2,128)(2,1)S(1)}, u32[]{:S(2)}, u32[]{:S(2)}) async-start(bf16[2,1024,512]{2,0,1:T(2,128)(2,1)} %bitcast.72), calls=%async_computation.1 | async-start | bytes 4194304 | tf_op jit(solution)/shard_map/all_to_all | solution.py:37
  11.7 2.5 convert_element_type.137
  14.2 3.5 %copy.78 = bf16[1,1,2,1024,512]{4,2,3,1,0:T(2,128)(2,1)} copy(bf16[1,1,2,1024,512]{4,3,2,1,0:T(8,128)(2,1)S(1)} %convert_element_type.137) | data formatting | bytes 4194304
  17.7 20.2 %all-to-all-done.1 = bf16[2,1024,512]{2,0,1:T(2,128)(2,1)S(1)} async-done(((bf16[2,1024,512]{2,0,1:T(2,128)(2,1)}), bf16[2,1024,512]{2,0,1:T(2,128)(2,1)S(1)}, u32[]{:S(2)}, u32[]{:S(2)}) %all-to-all-start.1) | async-done | bytes 2097184 | tf_op jit(solution)/shard_map/all_to_all | solution.py:37
  37.9 4.3 %all-to-all-start.3 = ((bf16[2,1024,512]{2,0,1:T(2,128)(2,1)}), bf16[2,1024,512]{2,0,1:T(2,128)(2,1)}, u32[]{:S(2)}, u32[]{:S(2)}) async-start(bf16[2,1024,512]{2,0,1:T(2,128)(2,1)} %bitcast.71), calls=%async_computation.3 | async-start | bytes 4194304 | tf_op jit(solution)/shard_map/all_to_all | solution.py:44
  42.3 5.1 %copy.81 = bf16[1,1,2,1024,512]{4,2,3,1,0:T(2,128)(2,1)} copy(bf16[1,1,2,1024,512]{4,3,2,1,0:T(8,128)(2,1)} %param.8) | data formatting | bytes 4194304 | tf_op args[0]
  47.3 21.1 %all-to-all-done.3 = bf16[2,1024,512]{2,0,1:T(2,128)(2,1)} async-done(((bf16[2,1024,512]{2,0,1:T(2,128)(2,1)}), bf16[2,1024,512]{2,0,1:T(2,128)(2,1)}, u32[]{:S(2)}, u32[]{:S(2)}) %all-to-all-start.3) | async-done | bytes 2097184 | tf_op jit(solution)/shard_map/all_to_all | solution.py:44
  68.4 4.3 %all-to-all-start = ((bf16[2,1024,512]{2,0,1:T(2,128)(2,1)}), bf16[2,1024,512]{2,0,1:T(2,128)(2,1)}, u32[]{:S(2)}, u32[]{:S(2)}) async-start(bf16[2,1024,512]{2,0,1:T(2,128)(2,1)} %bitcast.70), calls=%async_computation | async-start | bytes 4194304 | tf_op jit(solution)/shard_map/all_to_all | solution.py:36
  72.8 0.1 copy.53
  73.0 0.1 copy.54
  73.1 0.6 gather_fusion
  73.8 0.1 reshape.229
  73.9 0.7 gather_fusion.1
  74.7 0.2 convert_reduce_fusion.1
  74.9 0.7 gather_fusion.2
  75.8 5.1 %copy.80 = bf16[1,1,2,1024,512]{4,2,3,1,0:T(2,128)(2,1)} copy(bf16[1,1,2,1024,512]{4,3,2,1,0:T(8,128)(2,1)} %param.11) | data formatting | bytes 4194304 | tf_op args[3]
  81.0 18.0 %all-to-all-done = bf16[2,1024,512]{2,0,1:T(2,128)(2,1)} async-done(((bf16[2,1024,512]{2,0,1:T(2,128)(2,1)}), bf16[2,1024,512]{2,0,1:T(2,128)(2,1)}, u32[]{:S(2)}, u32[]{:S(2)}) %all-to-all-start) | async-done | bytes 2097184 | tf_op jit(solution)/shard_map/all_to_all | solution.py:36
  98.9 4.5 %all-to-all-start.2 = ((bf16[2,1024,512]{2,0,1:T(2,128)(2,1)}), bf16[2,1024,512]{2,0,1:T(2,128)(2,1)}, u32[]{:S(2)}, u32[]{:S(2)}) async-start(bf16[2,1024,512]{2,0,1:T(2,128)(2,1)} %bitcast.69), calls=%async_computation.2 | async-start | bytes 4194304 | tf_op jit(solution)/shard_map/all_to_all | solution.py:51
  103.6 0.1 reshape.243
  103.6 0.1 copy.55
  103.7 0.1 reshape.275
  103.8 0.3 copy.61
  104.2 0.6 convert_bitcast_fusion.3
  104.7 2.7 %copy.62 = f32[8,2,128,512]{3,2,1,0:T(8,128)} copy(f32[8,2,128,512]{3,2,0,1:T(8,128)S(1)} %convert_bitcast_fusion.3) | data formatting | bytes 8388608 | tf_op jit(solution)/shard_map/convert_element_type | solution.py:43
  107.5 1.9 copy.67
  109.4 0.6 convert_bitcast_fusion.2
  110.0 2.7 %copy.68 = f32[8,2,128,512]{3,2,1,0:T(8,128)} copy(f32[8,2,128,512]{3,2,0,1:T(8,128)S(1)} %convert_bitcast_fusion.2) | data formatting | bytes 8388608 | tf_op jit(solution)/shard_map/convert_element_type | solution.py:50
  112.7 2.9 %gather_fusion.4 = f32[12,128,512]{2,1,0:T(8,128)S(1)} fusion(f32[16,128,512]{2,1,0:T(8,128)} %bitcast.60, s32[1024]{0:T(1024)S(1)} %pad_clamp_fusion.1), kind=kCustom, calls=%fused_computation.4 | custom fusion | bytes 6291504 | tf_op jit(solution)/shard_map/gather | solution.py:73
  115.6 4.6 %gather_fusion.6 = f32[12,128,512]{2,1,0:T(8,128)} fusion(f32[16,128,512]{2,1,0:T(8,128)} %bitcast.61, s32[1024]{0:T(1024)S(1)} %pad_clamp_fusion.1), kind=kCustom, calls=%fused_computation.6 | custom fusion | bytes 6291504 | tf_op jit(solution)/shard_map/gather | solution.py:74
  120.2 1.9 copy.57
  122.2 1.5 copy.58
  123.7 3.5 %gather_fusion.3 = bf16[12,128,512]{2,1,0:T(8,128)(2,1)} fusion(bf16[16,128,512]{2,1,0:T(8,128)(2,1)} %bitcast.75, s32[1024]{0:T(1024)S(1)} %pad_clamp_fusion.1), kind=kCustom, calls=%fused_computation.3 | custom fusion | bytes 3145776 | tf_op jit(solution)/shard_map/gather | solution.py:72
  127.2 2.4 broadcast_multiply_fusion.1
  129.6 0.1 copy-done.2
  129.7 2.0 broadcast_multiply_fusion
  131.7 1.9 copy.64
  133.6 0.2 copy.65
  133.9 1.8 gather_fusion.5
  135.7 1.9 convert_reduce_fusion
  137.6 0.2 broadcast_multiply_fusion.2
  137.8 0.3 copy-done.3
  138.1 0.5 copy-done.4
  138.5 5.9 %fusion.2 = (bf16[4,3,128,512]{3,2,1,0:T(8,128)(2,1)}, f32[4,3,128,512]{3,2,1,0:T(8,128)S(1)}, f32[4,3,128,512]{3,2,1,0:T(8,128)}) fusion(bf16[4,3,128,512]{3,2,1,0:T(8,128)(2,1)S(1)} %bitcast.78, f32[4,3,128,512]{3,2,1,0:T(8,128)} %bitcast.65, f32[3,128,512]{2,1,0:T(8,128)S(1)} %get-tuple-element.9, f32[4,3,128,512]{3,2,1,0:T(8,128)S(1)} %bitcast.64, ...), kind=kLoop, calls=%fused_computation.18 | loop fusion | flops 7864320 | bytes 17301504 | tf_op jit(solution)/shard_map/convert_element_type | solution.py:78
  144.4 2.5 %broadcast.197.clone = f32[16,128,512]{2,1,0:T(8,128)} broadcast(f32[]{:T(128)} %constant.20.clone.1), dimensions={} | broadcast | bytes 4194308 | tf_op jit(solution)/shard_map/broadcast.10
  147.0 7.2 %scatter_fusion.1 = f32[16,128,512]{2,1,0:T(8,128)} fusion(f32[16,128,512]{2,1,0:T(8,128)} %broadcast.197.clone, s32[12]{0:T(128)S(1)} %reshape.275, f32[12,128,512]{2,1,0:T(8,128)} %bitcast.63), kind=kCustom, calls=%fused_computation.8 | custom fusion | bytes 9437232 | tf_op jit(solution)/shard_map/scatter | solution.py:81
  154.2 3.8 %convert_element_type.112 = bf16[16,128,512]{2,1,0:T(8,128)(2,1)} convert(f32[16,128,512]{2,1,0:T(8,128)} %scatter_fusion.1) | non-fusion elementwise | flops 1048576 | bytes 6291456 | tf_op jit(solution)/shard_map/convert_element_type | solution.py:86
  158.0 4.3 %all-to-all-start.5 = ((bf16[16,128,512]{2,1,0:T(8,128)(2,1)}), bf16[16,128,512]{2,1,0:T(8,128)(2,1)}, u32[]{:S(2)}, u32[]{:S(2)}) async-start(bf16[16,128,512]{2,1,0:T(8,128)(2,1)} %convert_element_type.112), calls=%async_computation.5 | async-start | bytes 4194304 | tf_op jit(solution)/shard_map/all_to_all | solution.py:85
  162.3 2.5 %broadcast.197.clone.1 = f32[16,128,512]{2,1,0:T(8,128)} broadcast(f32[]{:T(128)} %constant.20.clone.1), dimensions={} | broadcast | bytes 4194308 | tf_op jit(solution)/shard_map/broadcast.10
  164.9 6.1 %scatter_fusion.2 = f32[16,128,512]{2,1,0:T(8,128)} fusion(f32[16,128,512]{2,1,0:T(8,128)} %broadcast.197.clone.1, s32[12]{0:T(128)S(1)} %reshape.275, f32[12,128,512]{2,1,0:T(8,128)S(1)} %bitcast.62), kind=kCustom, calls=%fused_computation.9 | custom fusion | bytes 9437232 | tf_op jit(solution)/shard_map/scatter | solution.py:82
  170.9 3.8 %convert_element_type.117 = bf16[16,128,512]{2,1,0:T(8,128)(2,1)} convert(f32[16,128,512]{2,1,0:T(8,128)} %scatter_fusion.2) | non-fusion elementwise | flops 1048576 | bytes 6291456 | tf_op jit(solution)/shard_map/convert_element_type | solution.py:93
  174.7 13.7 %all-to-all-done.5 = bf16[16,128,512]{2,1,0:T(8,128)(2,1)} async-done(((bf16[16,128,512]{2,1,0:T(8,128)(2,1)}), bf16[16,128,512]{2,1,0:T(8,128)(2,1)}, u32[]{:S(2)}, u32[]{:S(2)}) %all-to-all-start.5) | async-done | bytes 2097184 | tf_op jit(solution)/shard_map/all_to_all | solution.py:85
  188.5 3.6 %all-to-all-start.6 = ((bf16[16,128,512]{2,1,0:T(8,128)(2,1)}), bf16[16,128,512]{2,1,0:T(8,128)(2,1)S(1)}, u32[]{:S(2)}, u32[]{:S(2)}) async-start(bf16[16,128,512]{2,1,0:T(8,128)(2,1)} %convert_element_type.117), calls=%async_computation.6 | async-start | bytes 4194304 | tf_op jit(solution)/shard_map/all_to_all | solution.py:92
  192.1 1.5 broadcast_in_dim.50
  193.6 5.5 %scatter_fusion = bf16[16,128,512]{2,1,0:T(8,128)(2,1)} fusion(bf16[16,128,512]{2,1,0:T(8,128)(2,1)} %broadcast_in_dim.50, s32[12]{0:T(128)S(1)} %reshape.275, bf16[12,128,512]{2,1,0:T(8,128)(2,1)} %bitcast.77), kind=kCustom, calls=%fused_computation.7 | custom fusion | bytes 4718640 | tf_op jit(solution)/shard_map/scatter | solution.py:80
  199.1 19.0 %all-to-all-done.6 = bf16[16,128,512]{2,1,0:T(8,128)(2,1)S(1)} async-done(((bf16[16,128,512]{2,1,0:T(8,128)(2,1)}), bf16[16,128,512]{2,1,0:T(8,128)(2,1)S(1)}, u32[]{:S(2)}, u32[]{:S(2)}) %all-to-all-start.6) | async-done | bytes 2097184 | tf_op jit(solution)/shard_map/all_to_all | solution.py:92
  218.2 4.3 %all-to-all-start.4 = ((bf16[16,128,512]{2,1,0:T(8,128)(2,1)}), bf16[16,128,512]{2,1,0:T(8,128)(2,1)}, u32[]{:S(2)}, u32[]{:S(2)}) async-start(bf16[16,128,512]{2,1,0:T(8,128)(2,1)} %scatter_fusion), calls=%async_computation.4 | async-start | bytes 4194304 | tf_op jit(solution)/shard_map/all_to_all | solution.py:84
  222.5 2.1 convert_bitcast_fusion.1
  224.7 2.7 %copy.70 = f32[2,8,128,512]{3,2,1,0:T(8,128)} copy(f32[2,8,128,512]{3,2,0,1:T(8,128)S(1)} %convert_bitcast_fusion.1) | data formatting | bytes 8388608 | tf_op jit(solution)/shard_map/convert_element_type | solution.py:91
  227.4 0.6 convert_bitcast_fusion
  228.0 2.7 %copy.71 = f32[2,8,128,512]{3,2,1,0:T(8,128)} copy(f32[2,8,128,512]{3,2,0,1:T(8,128)S(1)} %convert_bitcast_fusion) | data formatting | bytes 8388608 | tf_op jit(solution)/shard_map/convert_element_type | solution.py:98
  230.7 18.0 %all-to-all-done.4 = bf16[16,128,512]{2,1,0:T(8,128)(2,1)} async-done(((bf16[16,128,512]{2,1,0:T(8,128)(2,1)}), bf16[16,128,512]{2,1,0:T(8,128)(2,1)}, u32[]{:S(2)}, u32[]{:S(2)}) %all-to-all-start.4) | async-done | bytes 2097184 | tf_op jit(solution)/shard_map/all_to_all | solution.py:84
  248.7 3.1 %copy.69 = bf16[2,8,128,512]{3,2,1,0:T(8,128)(2,1)} copy(bf16[2,8,128,512]{3,2,0,1:T(8,128)(2,1)} %bitcast.24) | data formatting | bytes 4194304 | tf_op jit(solution)/shard_map/all_to_all | solution.py:84
  (25 shorter events, 0.6 us)
Async XLA Ops:
  6.6 31.3 %all-to-all-start.1 = ((bf16[2,1024,512]{2,0,1:T(2,128)(2,1)}), bf16[2,1024,512]{2,0,1:T(2,128)(2,1)S(1)}, u32[]{:S(2)}, u32[]{:S(2)}) async-start(bf16[2,1024,512]{2,0,1:T(2,128)(2,1)} %bitcast.72), calls=%async_computation.1 | async-start | bytes 4194304 | tf_op jit(solution)/shard_map/all_to_all | solution.py:37
  37.9 30.5 %all-to-all-start.3 = ((bf16[2,1024,512]{2,0,1:T(2,128)(2,1)}), bf16[2,1024,512]{2,0,1:T(2,128)(2,1)}, u32[]{:S(2)}, u32[]{:S(2)}) async-start(bf16[2,1024,512]{2,0,1:T(2,128)(2,1)} %bitcast.71), calls=%async_computation.3 | async-start | bytes 4194304 | tf_op jit(solution)/shard_map/all_to_all | solution.py:44
  47.3 25.5 %copy-start = (s32[4,3]{1,0:T(4,128)S(1)}, s32[4,3]{1,0:T(4,128)}, u32[]{:S(2)}) copy-start(s32[4,3]{1,0:T(4,128)} %param.12) | copy-start | bytes 148
  47.3 25.6 %copy-start.1 = (s32[4]{0:T(128)S(1)}, s32[4]{0:T(128)}, u32[]{:S(2)}) copy-start(s32[4]{0:T(128)} %param.14) | copy-start | bytes 52
  47.3 25.6 %copy-start.5 = (s32[3]{0:T(128)S(1)}, s32[3]{0:T(128)}, u32[]{:S(2)}) copy-start(s32[3]{0:T(128)} %param.13) | copy-start | bytes 40
  47.3 25.8 %copy-start.6 = (s32[3]{0:T(128)S(1)}, s32[3]{0:T(128)}, u32[]{:S(2)}) copy-start(s32[3]{0:T(128)} %param.15) | copy-start | bytes 40
  68.4 30.5 %all-to-all-start = ((bf16[2,1024,512]{2,0,1:T(2,128)(2,1)}), bf16[2,1024,512]{2,0,1:T(2,128)(2,1)}, u32[]{:S(2)}, u32[]{:S(2)}) async-start(bf16[2,1024,512]{2,0,1:T(2,128)(2,1)} %bitcast.70), calls=%async_computation | async-start | bytes 4194304 | tf_op jit(solution)/shard_map/all_to_all | solution.py:36
  98.9 32.8 %all-to-all-start.2 = ((bf16[2,1024,512]{2,0,1:T(2,128)(2,1)}), bf16[2,1024,512]{2,0,1:T(2,128)(2,1)}, u32[]{:S(2)}, u32[]{:S(2)}) async-start(bf16[2,1024,512]{2,0,1:T(2,128)(2,1)} %bitcast.69), calls=%async_computation.2 | async-start | bytes 4194304 | tf_op jit(solution)/shard_map/all_to_all | solution.py:51
  127.2 2.5 copy-start.2
  135.7 2.4 copy-start.3
  135.7 2.8 %copy-start.4 = (bf16[12,128,512]{2,1,0:T(8,128)(2,1)S(1)}, bf16[12,128,512]{2,1,0:T(8,128)(2,1)}, u32[]{:S(2)}) copy-start(bf16[12,128,512]{2,1,0:T(8,128)(2,1)} %gather_fusion.3) | copy-start | bytes 4718596
  158.0 30.5 %all-to-all-start.5 = ((bf16[16,128,512]{2,1,0:T(8,128)(2,1)}), bf16[16,128,512]{2,1,0:T(8,128)(2,1)}, u32[]{:S(2)}, u32[]{:S(2)}) async-start(bf16[16,128,512]{2,1,0:T(8,128)(2,1)} %convert_element_type.112), calls=%async_computation.5 | async-start | bytes 4194304 | tf_op jit(solution)/shard_map/all_to_all | solution.py:85
  188.5 29.7 %all-to-all-start.6 = ((bf16[16,128,512]{2,1,0:T(8,128)(2,1)}), bf16[16,128,512]{2,1,0:T(8,128)(2,1)S(1)}, u32[]{:S(2)}, u32[]{:S(2)}) async-start(bf16[16,128,512]{2,1,0:T(8,128)(2,1)} %convert_element_type.117), calls=%async_computation.6 | async-start | bytes 4194304 | tf_op jit(solution)/shard_map/all_to_all | solution.py:92
  218.2 30.5 %all-to-all-start.4 = ((bf16[16,128,512]{2,1,0:T(8,128)(2,1)}), bf16[16,128,512]{2,1,0:T(8,128)(2,1)}, u32[]{:S(2)}, u32[]{:S(2)}) async-start(bf16[16,128,512]{2,1,0:T(8,128)(2,1)} %scatter_fusion), calls=%async_computation.4 | async-start | bytes 4194304 | tf_op jit(solution)/shard_map/all_to_all | solution.py:84
where the time goes:
time: 253 us; the launch traced here: 252 us
  waiting for transfers between devices  110 us (43%)
  local copies, waits for them, and re-layouts  80.8 us (32%)
  starting transfers between devices  30.7 us (12%)
  other arithmetic  29.4 us (12%)
    all_to_all x1, waiting for transfers between devices, per_device(): lax.all_to_all(held_state[2].astype(jnp.bfloat16), ('pipe', 'section'), s...  21.1 us
    all_to_all x1, waiting for transfers between devices, per_device(): lax.all_to_all(held_state[1].astype(jnp.bfloat16), ('pipe', 'section'), s...  20.2 us
    all_to_all x1, waiting for transfers between devices, per_device(): lax.all_to_all(out_two.astype(jnp.bfloat16), ('pipe', 'section'), split_a...  19 us
    unnamed x19, local copies, waits for them, and re-layouts  18 us
    all_to_all x1, waiting for transfers between devices, per_device(): lax.all_to_all(out_weight, ('pipe', 'section'), split_axis=0, concat_axis...  18 us
    all_to_all x1, waiting for transfers between devices, per_device(): lax.all_to_all(held_state[0], ('pipe', 'section'), split_axis=1, concat_a...  18 us
    all_to_all x1, waiting for transfers between devices, per_device(): lax.all_to_all(out_one.astype(jnp.bfloat16), ('pipe', 'section'), split_a...  13.7 us
    scatter x1, local copies, waits for them, and re-layouts, per_device(): jnp.zeros(piece_one.shape, jnp.float32).at[place_index].set(next_one)  7.18 us
  transfers between devices with their start and end apart: 7, of which 6 were waited for; matrix products, arithmetic and copies ran while one was open for 30% of the time, Pallas kernels for 0%

commit v1 on v0

v1 whole, which is shorter than its diff:
```python
import math

import jax
import jax.numpy as jnp
from jax import lax
from jax.experimental import pallas as pl
from jax.experimental.pallas import tpu as pltpu
from jax.sharding import PartitionSpec as P

LEARN_RATE = 0.01
BETA_ONE = 0.9
BETA_TWO = 0.95
EPSILON = 1e-08
DECAY_RATE = 0.1

CORES = 2
TABLE = 8192
VMEM = 48 * 1024 * 1024
AXES = ("pipe", "section")


def both(*terms):
    out = terms[0]
    for term in terms[1:]:
        out = jnp.logical_and(out, term)
    return out


def as_int(flag):
    return jnp.where(flag, 1, 0).astype(jnp.int32)


def total(terms):
    out = jnp.int32(0)
    for term in terms:
        out = out + term
    return out


class Sizes:
    def __init__(self, weights, new_section):
        self.pipes = lax.axis_size("pipe")
        self.sections = lax.axis_size("section")
        self.groups = self.pipes // CORES
        self.slots = weights.shape[2]
        self.rows = weights.shape[3]
        self.cols = weights.shape[4]
        self.layers = new_section.shape[0]
        self.half = self.rows // CORES
        self.band = self.half // self.sections
        self.grad_band = self.half // self.groups
        doubles = self.layers - self.sections
        widest = 0
        for at in range(self.sections):
            low = at + max(0, doubles - (self.sections - at))
            high = min(self.layers - self.sections + at, at + min(at, doubles) + 1)
            widest = max(widest, high - low + 1)
        self.channels = min(widest, CORES * self.slots)

    def pairs(self, target):
        out = []
        for pipe in range(self.pipes):
            for section in range(self.sections):
                group, core, to = target(pipe // CORES, pipe % CORES, section)
                pipe_to = group * CORES + core
                out.append((pipe * self.sections + section, pipe_to * self.sections + to))
        return out

    def to_core(self, value):
        return lax.ppermute(value, AXES, self.pairs(lambda g, c, s: (g, 1 - c, s)))

    def to_group(self, value, shift):
        return lax.ppermute(value, AXES, self.pairs(lambda g, c, s: ((g + shift) % self.groups, c, s)))

    def to_section(self, value, shift):
        return lax.ppermute(value, AXES, self.pairs(lambda g, c, s: (g, c, (s + shift) % self.sections)))


def plan_tables(z, pipe, section, old, new, lost_pipe, offset):
    layers = range(z.layers)
    lost = lost_pipe(0)
    group, core = pipe // CORES, pipe % CORES
    sibling = group * CORES + (1 - core)
    lost_group = lost // CORES
    tables = {}

    def now_of(at):
        return [jnp.where(at == lost, new(l), old(at, l)) for l in layers]

    def slots_of(sections):
        return [total(as_int(sections[k] == sections[l]) for k in range(l)) for l in layers]

    def layer_at(sections, slots, at, slot):
        hits = [both(sections[l] == at, slots[l] == slot) for l in layers]
        index = total(jnp.where(hits[l], l, 0) for l in layers)
        return index, total(as_int(hit) for hit in hits)

    def lookup(values, index):
        out = values[0]
        for l in layers[1:]:
            out = jnp.where(index == l, values[l], out)
        return out

    my_now = now_of(pipe)
    my_slot = slots_of(my_now)
    sib_now = now_of(sibling)
    sib_slot = slots_of(sib_now)
    new_list = [new(l) for l in layers]
    new_slot = slots_of(new_list)

    def grad_unit(l, band):
        return [
            (as_int(my_now[l] == section), my_slot[l], core * z.groups + band),
            (as_int(sib_now[l] == section), sib_slot[l], band),
        ]

    for shift in range(1, z.groups):
        band = lax.rem(group + shift, z.groups)
        tables["grad_out", shift] = [grad_unit(l, band) for l in layers]
    tables["grad_sum"] = [
        grad_unit(l, group) + [(1, l, 0)] * (z.groups - 1) for l in layers
    ]
    tables["grad_mean"] = [[(1, l, 0)] * z.sections for l in layers]
    for name, sections, slots in (("mean_mine", my_now, my_slot), ("mean_sibling", sib_now, sib_slot)):
        units = []
        for slot in range(z.slots):
            index, found = layer_at(sections, slots, section, slot)
            for band in range(z.groups):
                unit = []
                for shift in range(z.groups):
                    from_group = lax.rem(group + z.groups - shift, z.groups)
                    unit.append((found * as_int(from_group == band), index, 0))
                units.append(unit)
        tables[name] = units

    donor = [lost_pipe(offset(l)) for l in layers]
    source_section = [old(donor[l], l) for l in layers]
    source_slot = [
        total(as_int(old(donor[l], k) == source_section[l]) for k in range(l)) for l in layers
    ]
    source_group = [donor[l] // CORES for l in layers]
    channel = [
        total(
            as_int(both(source_group[k] == source_group[l], source_section[k] == source_section[l]))
            for k in range(l)
        )
        for l in layers
    ]
    here = [as_int(source_group[l] == group) for l in layers]
    my_chip = [here[l] * as_int(source_section[l] == section) for l in layers]
    from_me = [as_int(donor[l] == pipe) for l in layers]
    slot_here = source_slot

    for shift in range(1, z.sections):
        band = lax.rem(section + shift, z.sections)
        units = []
        for k in range(z.channels):
            hit = [my_chip[l] * as_int(channel[l] == k) for l in layers]
            slot = total(hit[l] * slot_here[l] for l in layers)
            mine = total(hit[l] * from_me[l] for l in layers)
            found = total(hit)
            units.append([(mine, slot, core * z.sections + band), (found - mine, slot, band)])
        tables["spread", shift] = units

    def held(l_my_chip, l_from_me, l_slot, l_here, l_channel, l_section):
        unit = [
            (l_my_chip * l_from_me, l_slot, core * z.sections + section),
            (l_my_chip * (1 - l_from_me), l_slot, section),
        ]
        for shift in range(1, z.sections):
            sender = lax.rem(section + z.sections - shift, z.sections)
            unit.append((l_here * as_int(l_section == sender), l_channel, 0))
        return unit

    tables["across"] = [
        held(my_chip[l], from_me[l], slot_here[l], here[l], channel[l], source_section[l])
        for l in layers
    ]

    def arrived(index, found):
        unit = held(
            *(
                lookup(values, index)
                for values in (my_chip, from_me, slot_here, here, channel, source_section)
            )
        )
        unit = [(flag * found, at, block) for flag, at, block in unit]
        from_group = lookup(source_group, index)
        for shift in range(1, z.groups):
            sender = lax.rem(group + z.groups - shift, z.groups)
            unit.append((found * as_int(from_group == sender), index, 0))
        return unit

    for shift in range(1, z.sections):
        target = lax.rem(section + shift, z.sections)
        tables["deliver", shift] = [
            arrived(*layer_at(new_list, new_slot, target, slot)) for slot in range(z.slots)
        ]
    units = []
    for slot in range(z.slots):
        own = arrived(*layer_at(new_list, new_slot, section, slot))
        for band in range(z.sections):
            mine = as_int(section == band)
            unit = [(flag * mine, at, block) for flag, at, block in own]
            for shift in range(1, z.sections):
                sender = lax.rem(section + z.sections - shift, z.sections)
                unit.append((as_int(sender == band), slot, 0))
            units.append(unit)
    tables["collect"] = units

    last = [as_int(pipe == lost), core]
    for slot in range(z.slots):
        last.append(layer_at(my_now, my_slot, section, slot)[1])
    tables["update"] = [[tuple(last)]]
    return tables


def make_plan(z, old_section, new_section, lost_pipe, donor_offset):
    starts = {}
    place = jnp.stack([lax.axis_index("pipe"), lax.axis_index("section")]).astype(jnp.int32)

    def kernel(place_ref, old_ref, new_ref, lost_ref, offset_ref, table_ref):
        tables = plan_tables(
            z,
            place_ref[0],
            place_ref[1],
            lambda at, l: old_ref[at, l],
            lambda l: new_ref[l],
            lambda rank: lost_ref[rank],
            lambda l: offset_ref[l],
        )
        at = 0
        for name, units in tables.items():
            starts[name] = at
            for unit in units:
                for entry in unit:
                    for value in entry:
                        table_ref[at] = jnp.int32(value)
                        at += 1
        assert at <= TABLE

    smem = pl.BlockSpec(memory_space=pltpu.SMEM)
    table = pl.pallas_call(
        kernel,
        out_shape=jax.ShapeDtypeStruct((TABLE,), jnp.int32),
        in_specs=[smem] * 5,
        out_specs=smem,
        name="plan",
    )(place, old_section, new_section, lost_pipe, donor_offset)
    return table, starts


def pack(z, table, start, units, block, sources, name):
    count = len(sources)

    def entry(table_ref, unit, source, field):
        return table_ref[start + (unit * count + source) * 3 + field]

    def kernel(table_ref, *refs):
        unit = pl.program_id(0)
        out_ref = refs[-1]
        out = None
        for source, ref in enumerate(refs[:-1]):
            flag = entry(table_ref, unit, source, 0) != 0
            term = jnp.where(flag, ref[...].astype(jnp.float32), 0.0)
            out = term if out is None else out + term
        out_ref[...] = out.astype(out_ref.dtype)

    def index(source):
        def index_map(unit, table_ref):
            return (
                entry(table_ref, unit, source, 1),
                entry(table_ref, unit, source, 2),
                0,
            )

        return index_map

    moved = units * block * z.cols * (2 + sum(array.dtype.itemsize for array in sources))
    return pl.pallas_call(
        kernel,
        grid_spec=pltpu.PrefetchScalarGridSpec(
            num_scalar_prefetch=1,
            grid=(units,),
            in_specs=[pl.BlockSpec((1, block, z.cols), index(i)) for i in range(count)],
            out_specs=pl.BlockSpec((1, block, z.cols), lambda unit, table_ref: (unit, 0, 0)),
        ),
        out_shape=jax.ShapeDtypeStruct((units, block, z.cols), jnp.bfloat16),
        compiler_params=pltpu.CompilerParams(vmem_limit_bytes=VMEM),
        cost_estimate=pl.CostEstimate(
            flops=units * block * z.cols * count, bytes_accessed=moved, transcendentals=0
        ),
        name=name,
    )(table, *sources)


def update(z, table, start, state, rebuilt, mean):
    block = math.gcd(z.half, 256)
    per_half = z.half // block

    def kernel(table_ref, w_ref, one_ref, two_ref, *refs):
        mine_refs, other_refs = refs[:4], refs[4:8]
        out_w, out_one, out_two = refs[8:]
        slot, row = pl.program_id(0), pl.program_id(1)
        is_lost = table_ref[start] != 0
        mine = row // per_half == table_ref[start + 1]
        found = table_ref[start + 2 + slot] != 0

        def from_halves(at):
            return jnp.where(mine, mine_refs[at][...], other_refs[at][...]).astype(jnp.float32)

        grad = from_halves(3) * (1.0 / z.pipes)
        weight = jnp.where(is_lost, from_halves(0), w_ref[...].astype(jnp.float32))
        one = jnp.where(is_lost, from_halves(1), one_ref[...])
        two = jnp.where(is_lost, from_halves(2), two_ref[...])
        next_one = BETA_ONE * one + (1.0 - BETA_ONE) * grad
        next_two = BETA_TWO * two + (1.0 - BETA_TWO) * grad * grad
        step = next_one / (jnp.sqrt(next_two) + EPSILON) + DECAY_RATE * weight
        out_w[...] = jnp.where(found, weight - LEARN_RATE * step, 0.0).astype(out_w.dtype)
        out_one[...] = jnp.where(found, next_one, 0.0)
        out_two[...] = jnp.where(found, next_two, 0.0)

    def local(slot, row, table_ref):
        keep = 1 - table_ref[start]
        return (slot * keep, row * keep, 0)

    def half_of(own, needs_lost):
        def index_map(slot, row, table_ref):
            use = as_int((row // per_half == table_ref[start + 1]) == own)
            if needs_lost:
                use = use * table_ref[start]
            return (slot * use, lax.rem(row, per_half) * use, 0)

        return index_map

    def spec(index_map):
        return pl.BlockSpec((1, block, z.cols), index_map)

    def halves(own):
        return [spec(half_of(own, True))] * 3 + [spec(half_of(own, False))]

    shape = (z.slots, z.rows, z.cols)
    elements = z.slots * z.rows * z.cols
    return pl.pallas_call(
        kernel,
        grid_spec=pltpu.PrefetchScalarGridSpec(
            num_scalar_prefetch=1,
            grid=(z.slots, z.rows // block),
            in_specs=[spec(local)] * 3 + halves(True) + halves(False),
            out_specs=[spec(lambda slot, row, table_ref: (slot, row, 0))] * 3,
        ),
        out_shape=(
            jax.ShapeDtypeStruct(shape, jnp.bfloat16),
            jax.ShapeDtypeStruct(shape, jnp.float32),
            jax.ShapeDtypeStruct(shape, jnp.float32),
        ),
        compiler_params=pltpu.CompilerParams(vmem_limit_bytes=VMEM),
        cost_estimate=pl.CostEstimate(
            flops=elements * 14, bytes_accessed=elements * 22, transcendentals=elements * 2
        ),
        name="update",
    )(table, *state, *(r[0] for r in rebuilt), mean[0], *(r[1] for r in rebuilt), mean[1])


def per_device(
    weights,
    first_moment,
    second_moment,
    gradients,
    old_section,
    new_section,
    lost_pipe,
    donor_offset,
):
    z = Sizes(weights, new_section)
    core = lax.rem(lax.axis_index("pipe"), CORES)
    state = (weights[0, 0], first_moment[0, 0], second_moment[0, 0])
    grads = gradients[0, 0]

    def sibling_half(array):
        part = lax.dynamic_slice_in_dim(array, (1 - core) * z.half, z.half, axis=1)
        return z.to_core(part.astype(jnp.bfloat16))

    grads_sib = sibling_half(grads)
    state_sib = [sibling_half(array) for array in state]
    table, starts = make_plan(z, old_section, new_section, lost_pipe, donor_offset)

    def packed(name, units, block, sources):
        label = name if isinstance(name, str) else name[0]
        return pack(z, table, starts[name], units, block, sources, label)

    arrived = [
        z.to_group(packed(("grad_out", shift), z.layers, z.grad_band, [grads, grads_sib]), shift)
        for shift in range(1, z.groups)
    ]
    summed = packed("grad_sum", z.layers, z.grad_band, [grads, grads_sib] + arrived)
    others = [z.to_section(summed, shift) for shift in range(1, z.sections)]
    mean_band = packed("grad_mean", z.layers, z.grad_band, [summed] + others)
    bands = [mean_band] + [z.to_group(mean_band, shift) for shift in range(1, z.groups)]
    mean_units = z.slots * z.groups
    halves_shape = (z.slots, z.half, z.cols)
    mean_mine = packed("mean_mine", mean_units, z.grad_band, bands).reshape(halves_shape)
    mean_theirs = packed("mean_sibling", mean_units, z.grad_band, bands).reshape(halves_shape)
    mean = (mean_mine, z.to_core(mean_theirs))

    rebuilt = []
    for own, sib in zip(state, state_sib):
        held = [own, sib]
        for shift in range(1, z.sections):
            sent = packed(("spread", shift), z.channels, z.band, [own, sib])
            held.append(z.to_section(sent, shift))
        crossing = packed("across", z.layers, z.band, held)
        held = held + [z.to_group(crossing, shift) for shift in range(1, z.groups)]
        delivered = [
            z.to_section(packed(("deliver", shift), z.slots, z.band, held), shift)
            for shift in range(1, z.sections)
        ]
        half = packed("collect", z.slots * z.sections, z.band, held + delivered)
        half = half.reshape(halves_shape)
        rebuilt.append((half, z.to_core(half)))

    outs = update(z, table, starts["update"], state, rebuilt, mean)
    return tuple(out[None, None] for out in outs)


def solution(mesh):
    split = P("pipe", "section", None, "tp", None)
    return jax.shard_map(
        per_device,
        mesh=mesh,
        in_specs=(split,) * 4 + (P(),) * 4,
        out_specs=(split,) * 3,
        check_vma=False,
    )
```

time: 253 us -> 142 us (0.56)
  local copies, waits for them, and re-layouts: 80.8 us -> 15.1 us
  waiting for transfers between devices: 110 us -> 52.3 us
  Pallas kernels: 0 us -> 56.6 us
  other arithmetic: 29.4 us -> 0.55 us
  starting transfers between devices: 30.7 us -> 14.9 us
    all_to_all x7 -> x0, waiting for transfers between devices: 110 us -> none  [the longest x1 21.1 us: per_device(): lax.all_to_all(held_state[2].astype(jnp.bfloat16), ('pipe', 'section'), s...]
    pallas_call x0 -> x19, Pallas kernels: none -> 56.6 us  [the longest x17 41.6 us: pack(): pl.pallas_call(kernel, grid_spec=pltpu.PrefetchScalarGridSpec(num_scalar_...]
    ppermute x0 -> x20, waiting for transfers between devices: none -> 52.3 us  [the longest x7 33.1 us: to_section(): lax.ppermute(value, AXES, self.pairs(lambda g, c, s: (g, c, (s + shift) %...]
    all_to_all x7 -> x0, starting transfers between devices: 30.7 us -> none  [the longest x1 5.17 us: per_device(): lax.all_to_all(held_state[1].astype(jnp.bfloat16), ('pipe', 'section'), s...]
    convert_element_type x9 -> x0, other arithmetic: 22.2 us -> none  [the longest x1 5.9 us: per_device(): next_weight = (weight_now - LEARN_RATE * update).astype(jnp.bfloat16)]
    scatter x3 -> x0, local copies, waits for them, and re-layouts: 18.8 us -> none  [the longest x1 7.18 us: per_device(): jnp.zeros(piece_one.shape, jnp.float32).at[place_index].set(next_one)]
    gather x9 -> x0, local copies, waits for them, and re-layouts: 15.1 us -> none  [the longest x1 4.6 us: per_device(): moment_two = piece_two[source_index]]
    ppermute x0 -> x20, starting transfers between devices: none -> 14.9 us  [the longest x7 8 us: to_section(): lax.ppermute(value, AXES, self.pairs(lambda g, c, s: (g, c, (s + shift) %...]
  transfers between devices with their start and end apart: 7 -> 20, of which waited for: 6 -> 8; matrix products, arithmetic and copies ran while one was open for 30% -> 5% of each run, Pallas kernels for 0% -> 31%
where the time goes in v1:
time: 142 us; the launch traced here: 140 us
  Pallas kernels  56.6 us (40%)
  waiting for transfers between devices  52.3 us (37%)
  local copies, waits for them, and re-layouts  15.1 us (11%)
  starting transfers between devices  14.9 us (10%)
    pallas_call x17, Pallas kernels, pack(): pl.pallas_call(kernel, grid_spec=pltpu.PrefetchScalarGridSpec(num_scalar_...  41.6 us
    ppermute x7, waiting for transfers between devices, to_section(): lax.ppermute(value, AXES, self.pairs(lambda g, c, s: (g, c, (s + shift) %...  33.1 us
    ppermute x5, waiting for transfers between devices, to_group(): lax.ppermute(value, AXES, self.pairs(lambda g, c, s: ((g + shift) % self....  18.6 us
    pallas_call x1, Pallas kernels, update(): pl.pallas_call(kernel, grid_spec=pltpu.PrefetchScalarGridSpec(num_scalar_...  12.9 us
    ppermute x7, starting transfers between devices, to_section(): lax.ppermute(value, AXES, self.pairs(lambda g, c, s: (g, c, (s + shift) %...  8 us
    unnamed x18, local copies, waits for them, and re-layouts  6.29 us
    convert_element_type x2, local copies, waits for them, and re-layouts, sibling_half(): return z.to_core(part.astype(jnp.bfloat16))  5.39 us
    ppermute x5, starting transfers between devices, to_group(): lax.ppermute(value, AXES, self.pairs(lambda g, c, s: ((g + shift) % self....  5.13 us
  transfers between devices with their start and end apart: 20, of which 8 were waited for; matrix products, arithmetic and copies ran while one was open for 5% of the time, Pallas kernels for 31%

profile of v1, /device:TPU:0, one launch (start us, length us, event | category | flops | bytes accessed | tf_op | source)
XLA Modules:
  0.0 140.4 jit_solution(7695516289093874111)
XLA Ops:
  0.6 0.0 copy-start.2
  0.6 2.4 %dynamic-slice_bitcast_fusion = bf16[2,512,512]{2,1,0:T(8,128)(2,1)} fusion(bf16[1,1,2,1024,512]{4,3,2,1,0:T(8,128)(2,1)} %param.11, s32[]{:T(128)S(6)} %select_n.2), kind=kLoop, calls=%fused_computation.4 | loop fusion | bytes 2097156 | tf_op jit(solution)/shard_map/dynamic_slice | solution.py:381
  3.1 0.5 collective-permute-start.12
  3.5 2.7 %fusion.1 = bf16[2,512,512]{2,1,0:T(8,128)(2,1)} fusion(f32[1,1,2,1024,512]{4,3,2,1,0:T(8,128)} %param.10, s32[]{:T(128)S(6)} %select_n.2), kind=kLoop, calls=%fused_computation.3 | loop fusion | bytes 2097156 | tf_op jit(solution)/shard_map/convert_element_type | solution.py:382
  6.2 0.1 collective-permute-start.8
  6.3 2.7 %fusion = bf16[2,512,512]{2,1,0:T(8,128)(2,1)} fusion(f32[1,1,2,1024,512]{4,3,2,1,0:T(8,128)} %param.9, s32[]{:T(128)S(6)} %select_n.2), kind=kLoop, calls=%fused_computation.2 | loop fusion | bytes 2097156 | tf_op jit(solution)/shard_map/convert_element_type | solution.py:382
  9.0 0.5 collective-permute-start.4
  9.4 1.0 dynamic-slice_bitcast_fusion.1
  10.4 0.1 collective-permute-start
  10.5 0.6 pad_add_fusion.place_ref
  11.1 2.1 %plan.1.table_ref = s32[8192]{0:T(1024)} custom-call(s32[2]{0:T(128)} %pad_add_fusion.place_ref, s32[4,3]{1,0:T(4,128)} %old_ref.1, s32[3]{0:T(128)} %new_ref.1, s32[4]{0:T(128)} %lost_ref.1, s32[3]{0:T(128)} %offset_ref.1), custom_call_target="tpu_custom_call" | custom-call | tf_op jit(solution)/shard_map/plan/pallas_call | solution.py:243
  13.1 0.0 collective-permute-done.12.refs_1_
  13.2 0.0 copy-start.3
  13.2 1.6 %copy-done.3 = bf16[1,1,2,1024,512]{4,3,2,1,0:T(8,128)(2,1)S(1)} copy-done((bf16[1,1,2,1024,512]{4,3,2,1,0:T(8,128)(2,1)S(1)}, bf16[1,1,2,1024,512]{4,3,2,1,0:T(8,128)(2,1)}, u32[]{:S(2)}) %copy-start.3) | copy-done | bytes 2097176
  14.8 0.8 copy-done.5
  15.5 3.4 %grad_out.1 = bf16[3,256,512]{2,1,0:T(8,128)(2,1)S(1)} custom-call(s32[8192]{0:T(1024)S(1)} %copy-done.5, bf16[2,1024,512]{2,1,0:T(8,128)(2,1)S(1)} %bitcast.37, bf16[2,512,512]{2,1,0:T(8,128)(2,1)} %collective-permute-done.12.refs_1_), custom_call_target="tpu_custom_call" | custom-call | flops 786432 | bytes 2359296 | tf_op jit(solution)/shard_map/grad_out/pallas_call | solution.py:280
  18.9 3.0 %collective-permute-start.13 = (bf16[3,256,512]{2,1,0:T(8,128)(2,1)S(1)}, bf16[3,256,512]{2,1,0:T(8,128)(2,1)S(1)}, u32[]{:S(2)}, u32[]{:S(2)}) collective-permute-start(bf16[3,256,512]{2,1,0:T(8,128)(2,1)S(1)} %grad_out.1), channel_id=1, source_target_pairs={{0,16},{4,20},{8,24},{12,28},{16,0},{20,4},{24,8},{28,12},{1,17},{... | collective-permute-start | bytes 2359304 | tf_op jit(solution)/shard_map/ppermute | solution.py:73
  21.9 0.0 collective-permute-done.8.refs_1_
  21.9 2.2 %copy-done.1 = f32[1,1,2,1024,512]{4,3,2,1,0:T(8,128)S(1)} copy-done((f32[1,1,2,1024,512]{4,3,2,1,0:T(8,128)S(1)}, f32[1,1,2,1024,512]{4,3,2,1,0:T(8,128)}, u32[]{:S(2)}) %copy-start.1) | copy-done | bytes 4194328
  24.1 0.8 copy-done.6
  24.9 2.2 %spread.5 = bf16[2,256,512]{2,1,0:T(8,128)(2,1)S(1)} custom-call(s32[8192]{0:T(1024)S(1)} %copy-done.6, f32[2,1024,512]{2,1,0:T(8,128)S(1)} %bitcast.31, bf16[2,512,512]{2,1,0:T(8,128)(2,1)} %collective-permute-done.8.refs_1_), custom_call_target="tpu_custom_call" | custom-call | flops 524288 | bytes 2097152 | tf_op jit(solution)/shard_map/spread/pallas_call | solution.py:280
  27.1 1.6 %collective-permute-start.9 = (bf16[2,256,512]{2,1,0:T(8,128)(2,1)S(1)}, bf16[2,256,512]{2,1,0:T(8,128)(2,1)S(1)}, u32[]{:S(2)}, u32[]{:S(2)}) collective-permute-start(bf16[2,256,512]{2,1,0:T(8,128)(2,1)S(1)} %spread.5), channel_id=1, source_target_pairs={{0,4},{4,0},{8,12},{12,8},{16,20},{20,16},{24,28},{28,24},{1,5},{5... | collective-permute-start | bytes 1572872 | tf_op jit(solution)/shard_map/ppermute | solution.py:76
  28.7 2.2 %spread.4 = bf16[2,256,512]{2,1,0:T(8,128)(2,1)S(1)} custom-call(s32[8192]{0:T(1024)S(1)} %copy-done.6, f32[2,1024,512]{2,1,0:T(8,128)S(1)} %bitcast.26, bf16[2,512,512]{2,1,0:T(8,128)(2,1)} %collective-permute-done.4.refs_1_), custom_call_target="tpu_custom_call" | custom-call | flops 524288 | bytes 2097152 | tf_op jit(solution)/shard_map/spread/pallas_call | solution.py:280
  30.9 0.6 collective-permute-start.5
  31.5 0.0 collective-permute-done.refs_1_
  31.5 1.3 spread.3
  32.8 1.6 %collective-permute-start.1 = (bf16[2,256,512]{2,1,0:T(8,128)(2,1)S(1)}, bf16[2,256,512]{2,1,0:T(8,128)(2,1)S(1)}, u32[]{:S(2)}, u32[]{:S(2)}) collective-permute-start(bf16[2,256,512]{2,1,0:T(8,128)(2,1)S(1)} %spread.3), channel_id=1, source_target_pairs={{0,4},{4,0},{8,12},{12,8},{16,20},{20,16},{24,28},{28,24},{1,5},{5... | collective-permute-start | bytes 1572872 | tf_op jit(solution)/shard_map/ppermute | solution.py:76
  34.4 5.3 %collective-permute-done.13.refs_2_ = bf16[3,256,512]{2,1,0:T(8,128)(2,1)S(1)} collective-permute-done((bf16[3,256,512]{2,1,0:T(8,128)(2,1)S(1)}, bf16[3,256,512]{2,1,0:T(8,128)(2,1)S(1)}, u32[]{:S(2)}, u32[]{:S(2)}) %collective-permute-start.13) | collective-permute-done | bytes 786464 | tf_op jit(solution)/shard_map/ppermute | solution.py:73
  39.7 3.3 %grad_sum.1.refs_0_ = bf16[3,256,512]{2,1,0:T(8,128)(2,1)S(1)} custom-call(s32[8192]{0:T(1024)S(1)} %copy-done.6, bf16[2,1024,512]{2,1,0:T(8,128)(2,1)S(1)} %bitcast.38, bf16[2,512,512]{2,1,0:T(8,128)(2,1)} %collective-permute-done.12.refs_1_, bf16[3,256,512]{2,1,0:T(8,128)(2,1)S(1)} %collective-permute-done.13.refs_2_), custom_call_target="tpu_custom_call" | custom-call | flops 1179648 | bytes 3145728 | tf_op jit(solution)/shard_map/grad_sum/pallas_call | solution.py:280
  43.0 1.8 %collective-permute-start.14 = (bf16[3,256,512]{2,1,0:T(8,128)(2,1)S(1)}, bf16[3,256,512]{2,1,0:T(8,128)(2,1)S(1)}, u32[]{:S(2)}, u32[]{:S(2)}) collective-permute-start(bf16[3,256,512]{2,1,0:T(8,128)(2,1)S(1)} %grad_sum.1.refs_0_), channel_id=1, source_target_pairs={{0,4},{4,0},{8,12},{12,8},{16,20},{20,16},{24,28},{28,24},{1,5},{5... | collective-permute-start | bytes 2359304 | tf_op jit(solution)/shard_map/ppermute | solution.py:76
  44.8 3.6 %across.5 = bf16[3,256,512]{2,1,0:T(8,128)(2,1)S(1)} custom-call(s32[8192]{0:T(1024)S(1)} %copy-done.6, f32[2,1024,512]{2,1,0:T(8,128)} %bitcast.27, bf16[2,512,512]{2,1,0:T(8,128)(2,1)} %collective-permute-done.8.refs_1_, bf16[2,256,512]{2,1,0:T(8,128)(2,1)S(1)} %collective-permute-done.9.refs_2_), custom_call_target="tpu_custom_call" | custom-call | flops 1179648 | bytes 3932160 | tf_op jit(solution)/shard_map/across/pallas_call | solution.py:280
  48.4 1.6 %collective-permute-start.10 = (bf16[3,256,512]{2,1,0:T(8,128)(2,1)S(1)}, bf16[3,256,512]{2,1,0:T(8,128)(2,1)S(1)}, u32[]{:S(2)}, u32[]{:S(2)}) collective-permute-start(bf16[3,256,512]{2,1,0:T(8,128)(2,1)S(1)} %across.5), channel_id=1, source_target_pairs={{0,16},{4,20},{8,24},{12,28},{16,0},{20,4},{24,8},{28,12},{1,17},{... | collective-permute-start | bytes 2359304 | tf_op jit(solution)/shard_map/ppermute | solution.py:73
  50.0 3.3 %collective-permute-done.5.refs_2_ = bf16[2,256,512]{2,1,0:T(8,128)(2,1)S(1)} collective-permute-done((bf16[2,256,512]{2,1,0:T(8,128)(2,1)S(1)}, bf16[2,256,512]{2,1,0:T(8,128)(2,1)S(1)}, u32[]{:S(2)}, u32[]{:S(2)}) %collective-permute-start.5) | collective-permute-done | bytes 524320 | tf_op jit(solution)/shard_map/ppermute | solution.py:76
  53.2 3.6 %across.4 = bf16[3,256,512]{2,1,0:T(8,128)(2,1)S(1)} custom-call(s32[8192]{0:T(1024)S(1)} %copy-done.6, f32[2,1024,512]{2,1,0:T(8,128)} %bitcast.22, bf16[2,512,512]{2,1,0:T(8,128)(2,1)} %collective-permute-done.4.refs_1_, bf16[2,256,512]{2,1,0:T(8,128)(2,1)S(1)} %collective-permute-done.5.refs_2_), custom_call_target="tpu_custom_call" | custom-call | flops 1179648 | bytes 3932160 | tf_op jit(solution)/shard_map/across/pallas_call | solution.py:280
  56.9 0.1 collective-permute-start.6
  57.0 7.5 %collective-permute-done.1.refs_2_ = bf16[2,256,512]{2,1,0:T(8,128)(2,1)S(1)} collective-permute-done((bf16[2,256,512]{2,1,0:T(8,128)(2,1)S(1)}, bf16[2,256,512]{2,1,0:T(8,128)(2,1)S(1)}, u32[]{:S(2)}, u32[]{:S(2)}) %collective-permute-start.1) | collective-permute-done | bytes 524320 | tf_op jit(solution)/shard_map/ppermute | solution.py:76
  64.5 1.6 %across.3 = bf16[3,256,512]{2,1,0:T(8,128)(2,1)S(1)} custom-call(s32[8192]{0:T(1024)S(1)} %copy-done.6, bf16[2,1024,512]{2,1,0:T(8,128)(2,1)S(1)} %bitcast.34, bf16[2,512,512]{2,1,0:T(8,128)(2,1)S(1)} %collective-permute-done.refs_1_, bf16[2,256,512]{2,1,0:T(8,128)(2,1)S(1)} %collective-permute-done.1.refs_2_), custom_call_target="tpu_custom_call" | custom-call | flops 1179648 | bytes 3145728 | tf_op jit(solution)/shard_map/across/pallas_call | solution.py:280
  66.1 0.1 collective-permute-start.2
  66.2 13.9 %collective-permute-done.14.refs_1_ = bf16[3,256,512]{2,1,0:T(8,128)(2,1)S(1)} collective-permute-done((bf16[3,256,512]{2,1,0:T(8,128)(2,1)S(1)}, bf16[3,256,512]{2,1,0:T(8,128)(2,1)S(1)}, u32[]{:S(2)}, u32[]{:S(2)}) %collective-permute-start.14) | collective-permute-done | bytes 786464 | tf_op jit(solution)/shard_map/ppermute | solution.py:76
  80.1 1.4 %grad_mean.1.refs_0_ = bf16[3,256,512]{2,1,0:T(8,128)(2,1)S(1)} custom-call(s32[8192]{0:T(1024)S(1)} %copy-done.6, bf16[3,256,512]{2,1,0:T(8,128)(2,1)S(1)} %grad_sum.1.refs_0_, bf16[3,256,512]{2,1,0:T(8,128)(2,1)S(1)} %collective-permute-done.14.refs_1_), custom_call_target="tpu_custom_call" | custom-call | flops 786432 | bytes 2359296 | tf_op jit(solution)/shard_map/grad_mean/pallas_call | solution.py:280
  81.5 0.4 collective-permute-start.15
  81.9 0.0 collective-permute-done.10.refs_3_
  81.9 2.7 %deliver.5 = bf16[2,256,512]{2,1,0:T(8,128)(2,1)S(1)} custom-call(s32[8192]{0:T(1024)S(1)} %copy-done.6, f32[2,1024,512]{2,1,0:T(8,128)} %bitcast.28, bf16[2,512,512]{2,1,0:T(8,128)(2,1)} %collective-permute-done.8.refs_1_, bf16[2,256,512]{2,1,0:T(8,128)(2,1)S(1)} %collective-permute-done.9.refs_2_, bf16[3,256,512]{2,1,0:T(8,128)(2,1)S(1)} %collective-permute-done.10.refs_3_), custom_call_target="tpu_custom_call" | custom-call | flops 1048576 | bytes 3145728 | tf_op jit(solution)/shard_map/deliver/pallas_call | solution.py:280
  84.5 1.7 %collective-permute-start.11 = (bf16[2,256,512]{2,1,0:T(8,128)(2,1)S(1)}, bf16[2,256,512]{2,1,0:T(8,128)(2,1)S(1)}, u32[]{:S(2)}, u32[]{:S(2)}) collective-permute-start(bf16[2,256,512]{2,1,0:T(8,128)(2,1)S(1)} %deliver.5), channel_id=1, source_target_pairs={{0,4},{4,0},{8,12},{12,8},{16,20},{20,16},{24,28},{28,24},{1,5},{5... | collective-permute-start | bytes 1572872 | tf_op jit(solution)/shard_map/ppermute | solution.py:76
  86.3 2.7 %deliver.4 = bf16[2,256,512]{2,1,0:T(8,128)(2,1)S(1)} custom-call(s32[8192]{0:T(1024)S(1)} %copy-done.6, f32[2,1024,512]{2,1,0:T(8,128)} %bitcast.23, bf16[2,512,512]{2,1,0:T(8,128)(2,1)} %collective-permute-done.4.refs_1_, bf16[2,256,512]{2,1,0:T(8,128)(2,1)S(1)} %collective-permute-done.5.refs_2_, bf16[3,256,512]{2,1,0:T(8,128)(2,1)S(1)} %collective-permute-done.6.refs_3_), custom_call_target="tpu_custom_call" | custom-call | flops 1048576 | bytes 3145728 | tf_op jit(solution)/shard_map/deliver/pallas_call | solution.py:280
  89.0 0.4 collective-permute-start.7
  89.3 13.3 %collective-permute-done.2.refs_3_ = bf16[3,256,512]{2,1,0:T(8,128)(2,1)S(1)} collective-permute-done((bf16[3,256,512]{2,1,0:T(8,128)(2,1)S(1)}, bf16[3,256,512]{2,1,0:T(8,128)(2,1)S(1)}, u32[]{:S(2)}, u32[]{:S(2)}) %collective-permute-start.2) | collective-permute-done | bytes 786464 | tf_op jit(solution)/shard_map/ppermute | solution.py:73
  102.7 1.5 %deliver.3 = bf16[2,256,512]{2,1,0:T(8,128)(2,1)S(1)} custom-call(s32[8192]{0:T(1024)S(1)} %copy-done.6, bf16[2,1024,512]{2,1,0:T(8,128)(2,1)S(1)} %bitcast.35, bf16[2,512,512]{2,1,0:T(8,128)(2,1)S(1)} %collective-permute-done.refs_1_, bf16[2,256,512]{2,1,0:T(8,128)(2,1)S(1)} %collective-permute-done.1.refs_2_, ...), custom_call_target="tpu_custom_call" | custom-call | flops 1048576 | bytes 2621440 | tf_op jit(solution)/shard_map/deliver/pallas_call | solution.py:280
  104.2 0.4 collective-permute-start.3
  104.6 3.3 %collect.5 = bf16[4,256,512]{2,1,0:T(8,128)(2,1)S(1)} custom-call(s32[8192]{0:T(1024)S(1)} %copy-done.6, f32[2,1024,512]{2,1,0:T(8,128)} %bitcast.29, bf16[2,512,512]{2,1,0:T(8,128)(2,1)} %collective-permute-done.8.refs_1_, bf16[2,256,512]{2,1,0:T(8,128)(2,1)S(1)} %collective-permute-done.9.refs_2_, ...), custom_call_target="tpu_custom_call" | custom-call | flops 2621440 | bytes 7340032 | tf_op jit(solution)/shard_map/collect/pallas_call | solution.py:280
  107.9 0.1 collective-permute-start.18
  108.0 2.7 %collective-permute-done.7.refs_4_ = bf16[2,256,512]{2,1,0:T(8,128)(2,1)S(1)} collective-permute-done((bf16[2,256,512]{2,1,0:T(8,128)(2,1)S(1)}, bf16[2,256,512]{2,1,0:T(8,128)(2,1)S(1)}, u32[]{:S(2)}, u32[]{:S(2)}) %collective-permute-start.7) | collective-permute-done | bytes 524320 | tf_op jit(solution)/shard_map/ppermute | solution.py:76
  110.7 3.3 %collect.4 = bf16[4,256,512]{2,1,0:T(8,128)(2,1)S(1)} custom-call(s32[8192]{0:T(1024)S(1)} %copy-done.6, f32[2,1024,512]{2,1,0:T(8,128)} %bitcast.24, bf16[2,512,512]{2,1,0:T(8,128)(2,1)} %collective-permute-done.4.refs_1_, bf16[2,256,512]{2,1,0:T(8,128)(2,1)S(1)} %collective-permute-done.5.refs_2_, bf16[3,256,512]{2,1,0:T(8,128)(2,1)S(1)} %collective-permute-done.6.refs_3_, ...), custom_call_target="tpu_custom_call" | custom-call | flops 2621440 | bytes 7340032 | tf_op jit(solution)/shard_map/collect/pallas_call | solution.py:280
  114.0 0.1 collective-permute-start.17
  114.1 5.7 %collective-permute-done.3.refs_4_ = bf16[2,256,512]{2,1,0:T(8,128)(2,1)S(1)} collective-permute-done((bf16[2,256,512]{2,1,0:T(8,128)(2,1)S(1)}, bf16[2,256,512]{2,1,0:T(8,128)(2,1)S(1)}, u32[]{:S(2)}, u32[]{:S(2)}) %collective-permute-start.3) | collective-permute-done | bytes 524320 | tf_op jit(solution)/shard_map/ppermute | solution.py:76
  119.8 2.2 %collect.3 = bf16[4,256,512]{2,1,0:T(8,128)(2,1)S(1)} custom-call(s32[8192]{0:T(1024)S(1)} %copy-done.6, bf16[2,1024,512]{2,1,0:T(8,128)(2,1)S(1)} %bitcast.36, bf16[2,512,512]{2,1,0:T(8,128)(2,1)S(1)} %collective-permute-done.refs_1_, bf16[2,256,512]{2,1,0:T(8,128)(2,1)S(1)} %collective-permute-done.1.refs_2_, ...), custom_call_target="tpu_custom_call" | custom-call | flops 2621440 | bytes 6291456 | tf_op jit(solution)/shard_map/collect/pallas_call | solution.py:280
  122.0 0.1 collective-permute-start.16
  122.1 1.5 %mean_sibling.1 = bf16[4,256,512]{2,1,0:T(8,128)(2,1)S(1)} custom-call(s32[8192]{0:T(1024)S(1)} %copy-done.6, bf16[3,256,512]{2,1,0:T(8,128)(2,1)S(1)} %grad_mean.1.refs_0_, bf16[3,256,512]{2,1,0:T(8,128)(2,1)S(1)} %collective-permute-done.15.refs_1_), custom_call_target="tpu_custom_call" | custom-call | flops 1048576 | bytes 3145728 | tf_op jit(solution)/shard_map/mean_sibling/pallas_call | solution.py:280
  123.6 0.6 collective-permute-start.19
  124.2 1.5 %mean_mine.1 = bf16[4,256,512]{2,1,0:T(8,128)(2,1)S(1)} custom-call(s32[8192]{0:T(1024)S(1)} %copy-done.6, bf16[3,256,512]{2,1,0:T(8,128)(2,1)S(1)} %grad_mean.1.refs_0_, bf16[3,256,512]{2,1,0:T(8,128)(2,1)S(1)} %collective-permute-done.15.refs_1_), custom_call_target="tpu_custom_call" | custom-call | flops 1048576 | bytes 3145728 | tf_op jit(solution)/shard_map/mean_mine/pallas_call | solution.py:280
  125.8 0.7 collective-permute-done.19.refs_7_
  126.5 0.2 copy-done.7
  126.7 0.8 copy-done.8
  127.5 12.9 %update.1 = (bf16[2,1024,512]{2,1,0:T(8,128)(2,1)}, f32[2,1024,512]{2,1,0:T(8,128)}, f32[2,1024,512]{2,1,0:T(8,128)}) custom-call(s32[8192]{0:T(1024)S(1)} %copy-done.6, bf16[2,1024,512]{2,1,0:T(8,128)(2,1)} %bitcast.32, f32[2,1024,512]{2,1,0:T(8,128)} %bitcast.25, f32[2,1024,512]{2,1,0:T(8,128)} %bitcast.30, bf16[2,512,512]{2,1,0:T(8,128)(2,1)S(1)} %bitcast.40, ...), custom_call_target="tpu_custom_call" | custom-call | flops 14680064 | bytes 23068672 | tf_op jit(solution)/shard_map/update/pallas_call | solution.py:344
  (18 shorter events, 0.0 us)
Async XLA Ops:
  0.6 8.8 %copy-start.2 = (bf16[1,1,2,1024,512]{4,3,2,1,0:T(8,128)(2,1)S(1)}, bf16[1,1,2,1024,512]{4,3,2,1,0:T(8,128)(2,1)}, u32[]{:S(2)}) copy-start(bf16[1,1,2,1024,512]{4,3,2,1,0:T(8,128)(2,1)} %param.8) | copy-start | bytes 6291460
  3.1 10.1 %collective-permute-start.12 = (bf16[2,512,512]{2,1,0:T(8,128)(2,1)}, bf16[2,512,512]{2,1,0:T(8,128)(2,1)}, u32[]{:S(2)}, u32[]{:S(2)}) collective-permute-start(bf16[2,512,512]{2,1,0:T(8,128)(2,1)} %dynamic-slice_bitcast_fusion), channel_id=1, source_target_pairs={{0,8},{4,12},{8,0},{12,4},{16,24},{20,28},{24,16},{28,20},{1,9},{5... | collective-permute-start | bytes 3145736 | tf_op jit(solution)/shard_map/ppermute | solution.py:70
  6.2 15.7 %collective-permute-start.8 = (bf16[2,512,512]{2,1,0:T(8,128)(2,1)}, bf16[2,512,512]{2,1,0:T(8,128)(2,1)}, u32[]{:S(2)}, u32[]{:S(2)}) collective-permute-start(bf16[2,512,512]{2,1,0:T(8,128)(2,1)} %fusion.1), channel_id=1, source_target_pairs={{0,8},{4,12},{8,0},{12,4},{16,24},{20,28},{24,16},{28,20},{1,9},{5... | collective-permute-start | bytes 3145736 | tf_op jit(solution)/shard_map/ppermute | solution.py:70
  9.0 19.7 %collective-permute-start.4 = (bf16[2,512,512]{2,1,0:T(8,128)(2,1)}, bf16[2,512,512]{2,1,0:T(8,128)(2,1)}, u32[]{:S(2)}, u32[]{:S(2)}) collective-permute-start(bf16[2,512,512]{2,1,0:T(8,128)(2,1)} %fusion), channel_id=1, source_target_pairs={{0,8},{4,12},{8,0},{12,4},{16,24},{20,28},{24,16},{28,20},{1,9},{5... | collective-permute-start | bytes 3145736 | tf_op jit(solution)/shard_map/ppermute | solution.py:70
  10.4 21.1 %collective-permute-start = (bf16[2,512,512]{2,1,0:T(8,128)(2,1)}, bf16[2,512,512]{2,1,0:T(8,128)(2,1)S(1)}, u32[]{:S(2)}, u32[]{:S(2)}) collective-permute-start(bf16[2,512,512]{2,1,0:T(8,128)(2,1)} %dynamic-slice_bitcast_fusion.1), channel_id=1, source_target_pairs={{0,8},{4,12},{8,0},{12,4},{16,24},{20,28},{24,16},{28,20},{1,9},{5... | collective-permute-start | bytes 3145736 | tf_op jit(solution)/shard_map/ppermute | solution.py:70
  13.2 1.6 %copy-start.3 = (bf16[1,1,2,1024,512]{4,3,2,1,0:T(8,128)(2,1)S(1)}, bf16[1,1,2,1024,512]{4,3,2,1,0:T(8,128)(2,1)}, u32[]{:S(2)}) copy-start(bf16[1,1,2,1024,512]{4,3,2,1,0:T(8,128)(2,1)} %param.11) | copy-start | bytes 6291460
  14.8 0.8 copy-start.5
  15.5 13.2 %copy-start = (f32[1,1,2,1024,512]{4,3,2,1,0:T(8,128)S(1)}, f32[1,1,2,1024,512]{4,3,2,1,0:T(8,128)}, u32[]{:S(2)}) copy-start(f32[1,1,2,1024,512]{4,3,2,1,0:T(8,128)} %param.9) | copy-start | bytes 12582916
  18.9 20.7 %collective-permute-start.13 = (bf16[3,256,512]{2,1,0:T(8,128)(2,1)S(1)}, bf16[3,256,512]{2,1,0:T(8,128)(2,1)S(1)}, u32[]{:S(2)}, u32[]{:S(2)}) collective-permute-start(bf16[3,256,512]{2,1,0:T(8,128)(2,1)S(1)} %grad_out.1), channel_id=1, source_target_pairs={{0,16},{4,20},{8,24},{12,28},{16,0},{20,4},{24,8},{28,12},{1,17},{... | collective-permute-start | bytes 2359304 | tf_op jit(solution)/shard_map/ppermute | solution.py:73
  21.9 2.2 %copy-start.1 = (f32[1,1,2,1024,512]{4,3,2,1,0:T(8,128)S(1)}, f32[1,1,2,1024,512]{4,3,2,1,0:T(8,128)}, u32[]{:S(2)}) copy-start(f32[1,1,2,1024,512]{4,3,2,1,0:T(8,128)} %param.10) | copy-start | bytes 12582916
  24.1 0.8 copy-start.6
  27.1 17.7 %collective-permute-start.9 = (bf16[2,256,512]{2,1,0:T(8,128)(2,1)S(1)}, bf16[2,256,512]{2,1,0:T(8,128)(2,1)S(1)}, u32[]{:S(2)}, u32[]{:S(2)}) collective-permute-start(bf16[2,256,512]{2,1,0:T(8,128)(2,1)S(1)} %spread.5), channel_id=1, source_target_pairs={{0,4},{4,0},{8,12},{12,8},{16,20},{20,16},{24,28},{28,24},{1,5},{5... | collective-permute-start | bytes 1572872 | tf_op jit(solution)/shard_map/ppermute | solution.py:76
  28.7 11.0 %copy-start.4 = (bf16[1,1,2,1024,512]{4,3,2,1,0:T(8,128)(2,1)S(1)}, bf16[1,1,2,1024,512]{4,3,2,1,0:T(8,128)(2,1)}, u32[]{:S(2)}) copy-start(bf16[1,1,2,1024,512]{4,3,2,1,0:T(8,128)(2,1)} %param.11) | copy-start | bytes 6291460
  30.9 22.3 %collective-permute-start.5 = (bf16[2,256,512]{2,1,0:T(8,128)(2,1)S(1)}, bf16[2,256,512]{2,1,0:T(8,128)(2,1)S(1)}, u32[]{:S(2)}, u32[]{:S(2)}) collective-permute-start(bf16[2,256,512]{2,1,0:T(8,128)(2,1)S(1)} %spread.4), channel_id=1, source_target_pairs={{0,4},{4,0},{8,12},{12,8},{16,20},{20,16},{24,28},{28,24},{1,5},{5... | collective-permute-start | bytes 1572872 | tf_op jit(solution)/shard_map/ppermute | solution.py:76
  32.8 31.6 %collective-permute-start.1 = (bf16[2,256,512]{2,1,0:T(8,128)(2,1)S(1)}, bf16[2,256,512]{2,1,0:T(8,128)(2,1)S(1)}, u32[]{:S(2)}, u32[]{:S(2)}) collective-permute-start(bf16[2,256,512]{2,1,0:T(8,128)(2,1)S(1)} %spread.3), channel_id=1, source_target_pairs={{0,4},{4,0},{8,12},{12,8},{16,20},{20,16},{24,28},{28,24},{1,5},{5... | collective-permute-start | bytes 1572872 | tf_op jit(solution)/shard_map/ppermute | solution.py:76
  43.0 37.1 %collective-permute-start.14 = (bf16[3,256,512]{2,1,0:T(8,128)(2,1)S(1)}, bf16[3,256,512]{2,1,0:T(8,128)(2,1)S(1)}, u32[]{:S(2)}, u32[]{:S(2)}) collective-permute-start(bf16[3,256,512]{2,1,0:T(8,128)(2,1)S(1)} %grad_sum.1.refs_0_), channel_id=1, source_target_pairs={{0,4},{4,0},{8,12},{12,8},{16,20},{20,16},{24,28},{28,24},{1,5},{5... | collective-permute-start | bytes 2359304 | tf_op jit(solution)/shard_map/ppermute | solution.py:76
  48.4 33.5 %collective-permute-start.10 = (bf16[3,256,512]{2,1,0:T(8,128)(2,1)S(1)}, bf16[3,256,512]{2,1,0:T(8,128)(2,1)S(1)}, u32[]{:S(2)}, u32[]{:S(2)}) collective-permute-start(bf16[3,256,512]{2,1,0:T(8,128)(2,1)S(1)} %across.5), channel_id=1, source_target_pairs={{0,16},{4,20},{8,24},{12,28},{16,0},{20,4},{24,8},{28,12},{1,17},{... | collective-permute-start | bytes 2359304 | tf_op jit(solution)/shard_map/ppermute | solution.py:73
  56.9 29.4 %collective-permute-start.6 = (bf16[3,256,512]{2,1,0:T(8,128)(2,1)S(1)}, bf16[3,256,512]{2,1,0:T(8,128)(2,1)S(1)}, u32[]{:S(2)}, u32[]{:S(2)}) collective-permute-start(bf16[3,256,512]{2,1,0:T(8,128)(2,1)S(1)} %across.4), channel_id=1, source_target_pairs={{0,16},{4,20},{8,24},{12,28},{16,0},{20,4},{24,8},{28,12},{1,17},{... | collective-permute-start | bytes 2359304 | tf_op jit(solution)/shard_map/ppermute | solution.py:73
  66.1 36.6 %collective-permute-start.2 = (bf16[3,256,512]{2,1,0:T(8,128)(2,1)S(1)}, bf16[3,256,512]{2,1,0:T(8,128)(2,1)S(1)}, u32[]{:S(2)}, u32[]{:S(2)}) collective-permute-start(bf16[3,256,512]{2,1,0:T(8,128)(2,1)S(1)} %across.3), channel_id=1, source_target_pairs={{0,16},{4,20},{8,24},{12,28},{16,0},{20,4},{24,8},{28,12},{1,17},{... | collective-permute-start | bytes 2359304 | tf_op jit(solution)/shard_map/ppermute | solution.py:73
  81.5 40.6 %collective-permute-start.15 = (bf16[3,256,512]{2,1,0:T(8,128)(2,1)S(1)}, bf16[3,256,512]{2,1,0:T(8,128)(2,1)S(1)}, u32[]{:S(2)}, u32[]{:S(2)}) collective-permute-start(bf16[3,256,512]{2,1,0:T(8,128)(2,1)S(1)} %grad_mean.1.refs_0_), channel_id=1, source_target_pairs={{0,16},{4,20},{8,24},{12,28},{16,0},{20,4},{24,8},{28,12},{1,17},{... | collective-permute-start | bytes 2359304 | tf_op jit(solution)/shard_map/ppermute | solution.py:73
  84.5 20.0 %collective-permute-start.11 = (bf16[2,256,512]{2,1,0:T(8,128)(2,1)S(1)}, bf16[2,256,512]{2,1,0:T(8,128)(2,1)S(1)}, u32[]{:S(2)}, u32[]{:S(2)}) collective-permute-start(bf16[2,256,512]{2,1,0:T(8,128)(2,1)S(1)} %deliver.5), channel_id=1, source_target_pairs={{0,4},{4,0},{8,12},{12,8},{16,20},{20,16},{24,28},{28,24},{1,5},{5... | collective-permute-start | bytes 1572872 | tf_op jit(solution)/shard_map/ppermute | solution.py:76
  89.0 21.8 %collective-permute-start.7 = (bf16[2,256,512]{2,1,0:T(8,128)(2,1)S(1)}, bf16[2,256,512]{2,1,0:T(8,128)(2,1)S(1)}, u32[]{:S(2)}, u32[]{:S(2)}) collective-permute-start(bf16[2,256,512]{2,1,0:T(8,128)(2,1)S(1)} %deliver.4), channel_id=1, source_target_pairs={{0,4},{4,0},{8,12},{12,8},{16,20},{20,16},{24,28},{28,24},{1,5},{5... | collective-permute-start | bytes 1572872 | tf_op jit(solution)/shard_map/ppermute | solution.py:76
  104.2 15.6 %collective-permute-start.3 = (bf16[2,256,512]{2,1,0:T(8,128)(2,1)S(1)}, bf16[2,256,512]{2,1,0:T(8,128)(2,1)S(1)}, u32[]{:S(2)}, u32[]{:S(2)}) collective-permute-start(bf16[2,256,512]{2,1,0:T(8,128)(2,1)S(1)} %deliver.3), channel_id=1, source_target_pairs={{0,4},{4,0},{8,12},{12,8},{16,20},{20,16},{24,28},{28,24},{1,5},{5... | collective-permute-start | bytes 1572872 | tf_op jit(solution)/shard_map/ppermute | solution.py:76
  107.9 17.8 %collective-permute-start.18 = (bf16[2,512,512]{2,1,0:T(8,128)(2,1)S(1)}, bf16[2,512,512]{2,1,0:T(8,128)(2,1)S(1)}, u32[]{:S(2)}, u32[]{:S(2)}) collective-permute-start(bf16[2,512,512]{2,1,0:T(8,128)(2,1)S(1)} %bitcast.42), channel_id=1, source_target_pairs={{0,8},{4,12},{8,0},{12,4},{16,24},{20,28},{24,16},{28,20},{1,9},{5... | collective-permute-start | bytes 3145736 | tf_op jit(solution)/shard_map/ppermute | solution.py:70
  114.0 11.8 %collective-permute-start.17 = (bf16[2,512,512]{2,1,0:T(8,128)(2,1)S(1)}, bf16[2,512,512]{2,1,0:T(8,128)(2,1)}, u32[]{:S(2)}, u32[]{:S(2)}) collective-permute-start(bf16[2,512,512]{2,1,0:T(8,128)(2,1)S(1)} %bitcast.44), channel_id=1, source_target_pairs={{0,8},{4,12},{8,0},{12,4},{16,24},{20,28},{24,16},{28,20},{1,9},{5... | collective-permute-start | bytes 3145736 | tf_op jit(solution)/shard_map/ppermute | solution.py:70
  122.0 3.8 %collective-permute-start.16 = (bf16[2,512,512]{2,1,0:T(8,128)(2,1)S(1)}, bf16[2,512,512]{2,1,0:T(8,128)(2,1)S(1)}, u32[]{:S(2)}, u32[]{:S(2)}) collective-permute-start(bf16[2,512,512]{2,1,0:T(8,128)(2,1)S(1)} %bitcast.39), channel_id=1, source_target_pairs={{0,8},{4,12},{8,0},{12,4},{16,24},{20,28},{24,16},{28,20},{1,9},{5... | collective-permute-start | bytes 3145736 | tf_op jit(solution)/shard_map/ppermute | solution.py:70
  123.6 2.8 %collective-permute-start.19 = (bf16[2,512,512]{2,1,0:T(8,128)(2,1)S(1)}, bf16[2,512,512]{2,1,0:T(8,128)(2,1)S(1)}, u32[]{:S(2)}, u32[]{:S(2)}) collective-permute-start(bf16[2,512,512]{2,1,0:T(8,128)(2,1)S(1)} %bitcast.46), channel_id=1, source_target_pairs={{0,8},{4,12},{8,0},{12,4},{16,24},{20,28},{24,16},{28,20},{1,9},{5... | collective-permute-start | bytes 3145736 | tf_op jit(solution)/shard_map/ppermute | solution.py:70
  125.8 1.0 copy-start.7
  126.5 1.0 copy-start.8
